TPU v7x, 512 devices: a whole 4x4x16 slice. The times are simulated.
512 devices in a mesh: leaf: 32 (over z, core), sub: 16 (over y, x).
Axes of the slice: x: 4, y: 4, z: 16, core: 2. Of those that a mesh axis runs over, the one named last changes fastest.
Arguments:
- sources: float32 [16, 524288], P(None, ('leaf', 'sub')), may hold values from -6 to 6
- points: float32 [3, 524288], P(None, ('leaf', 'sub')), may hold values from -1 to 1
- basis: float32 [4096, 64, 128], P(('leaf', 'sub')), may hold values from -0.5 to 0.5
- leaf_transfer: float32 [4096, 4096], P(('leaf', 'sub')), may hold values from -1 to 1
- dev_transfer: float32 [512, 4096], P(('leaf', 'sub')), may hold values from -1 to 1
- leaf_coupling: float32 [4096, 8, 4096], P(('leaf', 'sub')), may hold values from -0.25 to 0.25
- dev_coupling: float32 [512, 8, 4096], P(('leaf', 'sub')), may hold values from -0.25 to 0.25
- grp_coupling: float32 [32, 8, 4096], P('leaf'), may hold values from -0.25 to 0.25
- near_list: int32 [4096, 8], P(('leaf', 'sub')), may hold values from 0 to 127
- leaf_far: int32 [4096, 8], P(('leaf', 'sub')), may hold values from 0 to 127
- dev_far: int32 [512, 8], P(('leaf', 'sub')), may hold values from 0 to 511
- grp_far: int32 [32, 8], P('leaf'), may hold values from 0 to 31
Outputs:
- product: float32 [16, 524288], P(None, ('leaf', 'sub'))
Inputs may be any that keep to these rules, and one draw needn't show every extreme that they name: Leaf numbers in near_list and leaf_far count within the subtree of the leaf that lists them; entries may repeat. `leaf_far`: entries may repeat. `dev_far`: entries may repeat. `grp_far`: entries may repeat.
All inputs are finite; a program needn't handle non-finite values.
Results may differ from a plain program's by a relative error of at most 0.0001.
Values sent between devices are 32-bit elements; how exact they have to be, the bound alone decides.
A program may use at most 64 MiB of HBM per device.

v0:
```python
import math

import jax
import jax.numpy as jnp
from jax import lax
from jax.sharding import PartitionSpec as P

delta_sq = 0.01


def kernel_block(targets, sources):
    along_x = targets[0][:, :, None] - sources[0][:, None, :]
    along_y = targets[1][:, :, None] - sources[1][:, None, :]
    along_z = targets[2][:, :, None] - sources[2][:, None, :]
    return 1.0 / jnp.sqrt(along_x * along_x + along_y * along_y + along_z * along_z + delta_sq)


def body(
    sources,
    points,
    basis,
    leaf_transfer,
    dev_transfer,
    leaf_coupling,
    dev_coupling,
    grp_coupling,
    near_list,
    leaf_far,
    dev_far,
    grp_far,
):
    highest = lax.Precision.HIGHEST
    count_leaf = basis.shape[0]
    rank_size = basis.shape[1]
    leaf_size = basis.shape[2]
    vector_count = sources.shape[0]
    sub_count = lax.axis_size("sub")
    signal = sources.reshape(vector_count, count_leaf, leaf_size)
    leaf_coef = jnp.einsum("tal,vtl->tva", basis, signal, precision=highest)
    leaf_maps = leaf_transfer.reshape(count_leaf, rank_size, rank_size)
    dev_coef = jnp.einsum("tab,tvb->va", leaf_maps, leaf_coef, precision=highest)
    dev_map = dev_transfer.reshape(rank_size, rank_size)
    up_term = jnp.einsum("ab,vb->va", dev_map, dev_coef, precision=highest)
    dev_pairs = dev_coupling.reshape(dev_far.shape[1], rank_size, rank_size)
    partner_devices = dev_far[0]
    grp_coef = lax.psum(up_term, "sub")
    grp_all = lax.all_gather(grp_coef[None], "leaf", axis=0, tiled=True)
    shard_rows = lax.all_gather(dev_coef[None], ("leaf", "sub"), axis=0, tiled=True)
    indices = jnp.arange(shard_rows.shape[0], dtype=jnp.int32)
    matches = (partner_devices[:, None] == indices[None, :]).astype(jnp.float32)
    selected = jnp.einsum("kn,nva->kva", matches, shard_rows, precision=highest)
    dev_local = jnp.einsum("kab,kvb->va", dev_pairs, selected, precision=highest)
    grp_pairs = grp_coupling.reshape(grp_far.shape[1], rank_size, rank_size)
    grp_local = jnp.einsum("kab,kvb->va", grp_pairs, grp_all[grp_far[0]], precision=highest)
    dev_total = dev_local + jnp.einsum("ab,va->vb", dev_map, grp_local, precision=highest)
    group_signal, group_points = (
        lax.all_gather(sources, "sub", axis=1, tiled=True),
        lax.all_gather(points, "sub", axis=1, tiled=True),
    )
    leaf_pairs = leaf_coupling.reshape(count_leaf, leaf_far.shape[1], rank_size, rank_size)
    shard_rows = lax.all_gather(leaf_coef, "sub", axis=0, tiled=True)
    indices = jnp.arange(shard_rows.shape[0], dtype=jnp.int32)
    matches = (leaf_far[:, :, None] == indices[None, None, :]).astype(jnp.float32)
    selected = jnp.einsum("tkn,nva->tkva", matches, shard_rows, precision=highest)
    far_local = jnp.einsum("tkab,tkvb->tva", leaf_pairs, selected, precision=highest)
    leaf_total = far_local + jnp.einsum("tab,va->tvb", leaf_maps, dev_total, precision=highest)
    far_field = jnp.einsum("tal,tva->vtl", basis, leaf_total, precision=highest)
    group_leaves = count_leaf * sub_count
    signal_all = group_signal.reshape(vector_count, group_leaves, leaf_size)
    points_all = group_points.reshape(3, group_leaves, leaf_size)
    own_points = points.reshape(3, count_leaf, leaf_size)

    def near_step(position, running):
        source_leaves = lax.dynamic_index_in_dim(near_list, position, 1, keepdims=False)
        kernel_tile = kernel_block(own_points, points_all[:, source_leaves, :])
        return running + jnp.einsum(
            "tpq,vtq->vtp", kernel_tile, signal_all[:, source_leaves, :], precision=highest
        )

    near_field = lax.fori_loop(
        0,
        near_list.shape[1],
        near_step,
        jnp.zeros((vector_count, count_leaf, leaf_size), jnp.float32),
    )
    near_weight = 1.0 / math.sqrt(near_list.shape[1] * leaf_size)
    return (far_field + near_weight * near_field).reshape(vector_count, count_leaf * leaf_size)


def solution(mesh):
    placed = (
        P(None, ("leaf", "sub")),
        P(None, ("leaf", "sub")),
        P(("leaf", "sub"), None, None),
        P(("leaf", "sub"), None),
        P(("leaf", "sub"), None),
        P(("leaf", "sub"), None, None),
        P(("leaf", "sub"), None, None),
        P("leaf", None, None),
        P(("leaf", "sub"), None),
        P(("leaf", "sub"), None),
        P(("leaf", "sub"), None),
        P("leaf", None),
    )
    return jax.shard_map(
        body, mesh=mesh, in_specs=placed, out_specs=P(None, ("leaf", "sub")), check_vma=False
    )
```

profile of v0, /device:TPU:1, one launch (start us, length us, event | category | flops | bytes accessed | tf_op | source)
XLA Modules:
  0.0 288.8 jit_solution(2543322029373095318)
XLA Ops:
  8.3 1.4 fusion.31
  10.7 21.1 %all_gather.15 = f32[128,16,64]{2,1,0:T(8,128)S(1)} all-gather(f32[8,16,64]{2,1,0:T(8,128)S(1)} %fusion.31), channel_id=1, replica_groups=mesh['leaf'=32,'sub'=16] {'sub'}, dimensions={0}, use_global_device_ids=true | all-gather | bytes 557056 | tf_op jit(solution)/shard_map/all_gather | solution.py:61
  32.4 1.4 reduce.3
  34.8 31.4 %psum.7 = f32[1,16,64]{2,1,0:T(8,128)S(1)} all-reduce(f32[1,16,64]{2,1,0:T(8,128)S(1)} %convolution_bitcast_fusion.5), channel_id=1, replica_groups=mesh['leaf'=32,'sub'=16] {'sub'}, use_global_device_ids=true, to_apply=%region_0.0 | all-reduce | flops 1024 | bytes 8192 | tf_op jit(solution)/shard_map/psum | solution.py:46
  66.2 52.7 %all_gather.17 = f32[32,16,64]{2,1,0:T(8,128)} all-gather(f32[1,16,64]{2,1,0:T(8,128)S(1)} %psum.7), channel_id=1, replica_groups=mesh['leaf'=32,'sub'=16] {'leaf'}, dimensions={0}, use_global_device_ids=true | all-gather | bytes 135168 | tf_op jit(solution)/shard_map/all_gather | solution.py:47
  119.6 1.7 reshape.71
  121.3 1.7 reshape.69
  123.1 2.0 reshape.67
  125.1 18.0 %all_gather.19 = f32[3,16384]{1,0:T(4,128)} all-gather(f32[3,1024]{1,0:T(4,128)S(1)} %copy-done.5), channel_id=1, replica_groups=mesh['leaf'=32,'sub'=16] {'sub'}, dimensions={1}, use_global_device_ids=true | all-gather | bytes 208896 | tf_op jit(solution)/shard_map/all_gather | solution.py:58
  143.1 1.5 gather_fusion.2
  144.6 1.2 convolution_bitcast_fusion.4
  146.7 1.9 convolution_bitcast_fusion.3
  148.6 1.3 copy_bitcast_fusion
  149.9 27.5 %while.14 = (s32[]{:T(128)}, f32[16,8,128]{2,0,1:T(8,128)S(1)}, s32[8,8]{0,1:T(8,128)S(1)}, f32[16,128,128]{2,0,1:T(8,128)S(1)}, f32[3,8,128]{2,1,0:T(8,128)S(1)...) while((s32[]{:T(128)}, f32[16,8,128]{2,0,1:T(8,128)S(1)}, s32[8,8]{0,1:T(8,128)S(1)}, ...), condition=%wide.region_2.3_spmd.clone, body=%wide.region_1.2_spmd.clone.sunk | while | flops 26379292 | bytes 430339 | solution.py:80
  150.0 1.5 gather_fusion
  152.1 1.3 fusion.69
  153.4 1.5 gather_fusion
  155.5 1.3 fusion.69
  156.8 1.5 gather_fusion
  159.0 1.3 fusion.69
  160.3 1.5 gather_fusion
  162.4 1.3 fusion.69
  163.7 1.5 gather_fusion
  165.8 1.3 fusion.69
  167.1 1.5 gather_fusion
  169.3 1.3 fusion.69
  170.6 1.5 gather_fusion
  172.7 1.3 fusion.69
  174.0 1.5 gather_fusion
  176.1 1.3 fusion.69
  177.4 98.2 %all-gather.6.cloned.1.call-done = f32[8192,64]{1,0:T(8,128)} async-done(((f32[16,64]{1,0:T(8,128)}), f32[8192,64]{1,0:T(8,128)}) %all-gather.6.cloned.1.call-update) | async-done | bytes 2097168 | tf_op jit(solution)/shard_map/all_gather | solution.py:48
  275.6 4.6 %fusion.21 = f32[8,16,64]{2,0,1:T(8,128)S(1)} fusion(f32[512,16,64]{2,1,0:T(8,128)} %bitcast.112, s32[8]{0:T(128)S(1)} %bitcast.120), kind=kOutput, calls=%fused_computation.30 | convolution fusion | flops 50335744 | bytes 2129952 | tf_op jit(solution)/shard_map/kn,nva->kva/dot_general | solution.py:51
  (79 shorter events, 12.1 us)
Async XLA Ops:
  6.5 1.8 copy-start
  6.5 118.5 %copy-start.5 = (f32[3,1024]{1,0:T(4,128)S(1)}, f32[3,1024]{1,0:T(4,128)}, u32[]{:S(2)}) copy-start(f32[3,1024]{1,0:T(4,128)} %param.15) | copy-start | bytes 36868
  6.5 136.5 %copy-start.7 = (s32[8,8]{1,0:T(8,128)S(1)}, s32[8,8]{1,0:T(8,128)}, u32[]{:S(2)}) copy-start(s32[8,8]{1,0:T(8,128)} %param.22) | copy-start | bytes 772
  6.5 139.3 %copy-start.6 = (s32[8,8]{1,0:T(8,128)S(1)}, s32[8,8]{1,0:T(8,128)}, u32[]{:S(2)}) copy-start(s32[8,8]{1,0:T(8,128)} %param.23) | copy-start | bytes 772
  6.5 142.0 %all-gather.4.cloned.1.call-start = ((), (), s32[]{:S(2)}) async-start(), calls=%async_computation | async-start | bytes 1114112 | tf_op jit(solution)/shard_map/all_gather | solution.py:57
  7.3 268.3 %all-gather.6.cloned.1.call-start = ((), (), s32[]{:S(2)}) async-start(), calls=%async_computation.1 | async-start | bytes 4202496 | tf_op jit(solution)/shard_map/all_gather | solution.py:48
  8.3 113.0 %copy-start.1 = (f32[8,64,64]{2,1,0:T(8,128)}, f32[8,64,64]{2,1,0:T(8,128)S(1)}, u32[]{:S(2)}) copy-start(f32[8,64,64]{2,1,0:T(8,128)S(1)} %reshape.68) | copy-start | bytes 393220
  145.9 4.0 %copy-start.4 = (f32[16,8,128]{2,0,1:T(8,128)S(1)}, f32[16,8,128]{2,0,1:T(8,128)}, u32[]{:S(2)}) copy-start(f32[16,8,128]{2,0,1:T(8,128)} %custom-call) | copy-start | bytes 196612
  149.9 125.7 %copy-start.8 = (s32[1,8]{1,0:T(1,128)S(1)}, s32[1,8]{1,0:T(1,128)}, u32[]{:S(2)}) copy-start(s32[1,8]{1,0:T(1,128)} %param.24) | copy-start | bytes 100
  177.4 102.9 %copy-start.3 = (f32[8,64,64]{2,1,0:T(8,128)S(1)}, f32[8,64,64]{2,1,0:T(8,128)}, u32[]{:S(2)}) copy-start(f32[8,64,64]{2,1,0:T(8,128)} %reshape.69) | copy-start | bytes 393220
  177.4 103.3 %copy-start.2 = (f32[8,64,64]{2,1,0:T(8,128)S(1)}, f32[8,64,64]{2,1,0:T(8,128)}, u32[]{:S(2)}) copy-start(f32[8,64,64]{2,1,0:T(8,128)} %copy-done.1) | copy-start | bytes 393220
Sparse Core Ops, SparseCore 0:
  10.4 61.8 all-gather.3
  76.7 198.8 all-gather.5
where the time goes:
time: 290 us; the launch traced here: 289 us
  blocking collectives  123 us (42%)
  waiting for transfers between devices  98.9 us (34%)
  local copies, waits for them, and re-layouts  27.4 us (9%)
  matrix products  22.9 us (8%)
  between operations  13.6 us (5%)
    all_gather x1, waiting for transfers between devices, body(): lax.all_gather(dev_coef[None], ('leaf', 'sub'), axis=0, tiled=True)  98.2 us
    all_gather x1, blocking collectives, body(): grp_all = lax.all_gather(grp_coef[None], 'leaf', axis=0, tiled=True)  52.7 us
    psum x1, blocking collectives, body(): grp_coef = lax.psum(up_term, 'sub')  31.4 us
    all_gather x1, blocking collectives, body(): shard_rows = lax.all_gather(leaf_coef, 'sub', axis=0, tiled=True)  21.1 us
    all_gather x1, blocking collectives, body(): lax.all_gather(points, 'sub', axis=1, tiled=True)  18 us
    gather x8, local copies, waits for them, and re-layouts, near_step(): kernel_tile = kernel_block(own_points, points_all[:, source_leaves, :])  12.2 us
    dot_general x8, matrix products, near_step(): jnp.einsum('tpq,vtq->vtp', kernel_tile, signal_all[:, source_leaves, :],...  10.1 us
  transfers between devices with their start and end apart: 2, of which 1 were waited for; matrix products, arithmetic and copies ran while one was open for 16% of the time, Pallas kernels for 0%

commit v1 on v0

v1 whole, which is shorter than its diff:
```python
import jax
import jax.numpy as jnp
from jax import lax
from jax.experimental import pallas as pl
from jax.experimental.pallas import tpu as pltpu
from jax.sharding import PartitionSpec as P

MESH = pl.DeviceIdType.MESH
F32, BF16 = jnp.float32, jnp.bfloat16
DELTA_SQ = 0.01
NZ, NSUB, SIDE = 16, 16, 4
LEAVES_DEV, NEAR, FAR = 8, 8, 8
HALF_TILES = 14
NEAR_WEIGHT = 1.0 / 32.0
NT = ((1,), (1,))
NN = ((1,), (0,))


def split(x):
    high = x.astype(BF16)
    return high, (x - high.astype(F32)).astype(BF16)


def dot(a, b, dims):
    return lax.dot_general(a, b, (dims, ((), ())), preferred_element_type=F32)


def dot3(a, b, dims):
    return dot(a[0], b[0], dims) + (dot(a[1], b[0], dims) + dot(a[0], b[1], dims))


def kernel(
    src, pts, basis, e_hbm, f_hbm, lc_hbm, dc_hbm, gc_hbm, near_hbm, lfar_hbm, dfar_hbm, gfar_hbm,
    out,
    src_v, pts_v, basis_v, e_v, f_v, lc_v, dc_v, gc_v, dfar_v, near_s, lfar_s, gfar_s,
    w_h, w_l, rf_h, rf_l, rd_h, rd_l, rg_h, rg_l, perm_v, cols_v, acc,
    gat, table, req_v, req_s, r_out, r_in, p_out, p_in,
    loc_sem, gat_send, gat_recv, z_send, z_recv, c_sem, req_send, req_recv, req_loc, r_send, r_recv, p_send, p_recv,
):
    leaf = lax.axis_index("leaf")
    sub = lax.axis_index("sub")
    z, core = leaf // 2, lax.rem(leaf, 2)
    y, x = sub // SIDE, lax.rem(sub, SIDE)

    def at_plane(dy, dx):
        return lax.rem(y + dy, SIDE) * SIDE + lax.rem(x + dx, SIDE)

    plane = [at_plane(d // SIDE, d % SIDE) for d in range(1, NSUB)]
    others = [i + (i >= z).astype(jnp.int32) for i in range(NZ - 1)]
    mate = (leaf + 1 - 2 * core, sub)

    pairs = [
        (basis, basis_v), (e_hbm, e_v), (src, src_v), (f_hbm, f_v), (pts, pts_v), (dfar_hbm, dfar_v), (near_hbm, near_s),
        (lfar_hbm, lfar_s), (gfar_hbm, gfar_s), (dc_hbm, dc_v), (gc_hbm, gc_v), (lc_hbm, lc_v),
    ]
    loads = [pltpu.make_async_copy(a, b, loc_sem.at[i]) for i, (a, b) in enumerate(pairs)]
    for c in loads:
        c.start()
    barrier = pltpu.get_barrier_semaphore()
    for o in others:
        pl.semaphore_signal(barrier, inc=1, device_id=(o * 2 + core, sub), device_id_type=MESH)
    for o in plane:
        pl.semaphore_signal(barrier, inc=1, device_id=(leaf, o), device_id_type=MESH)
    pl.semaphore_signal(barrier, inc=1, device_id=mate, device_id_type=MESH)

    lane = lax.broadcasted_iota(jnp.int32, (1, 128), 1)
    left = lane < 64

    def keep(part, value):
        return jnp.where(left if part == 0 else jnp.logical_not(left), value, 0.0)

    def stack(value):
        return jnp.concatenate([keep(0, value), keep(1, value)], axis=0)

    def twice(value):
        return jnp.concatenate([value, value], axis=0)

    def pack(value):
        return jnp.where(left, value[0:8], value[8:16])

    def spread(value):
        turned = pltpu.roll(value, 64, 1)
        return jnp.concatenate([jnp.where(left, value, turned), jnp.where(left, turned, value)], axis=0)

    row_i = lax.broadcasted_iota(jnp.int32, (128, 128), 0)
    col_i = lax.broadcasted_iota(jnp.int32, (128, 128), 1)
    wanted = (col_i // 64) * 64 + 2 * lax.rem(col_i, 32) + lax.rem(col_i // 32, 2)
    perm_v[...] = (row_i == wanted).astype(F32).astype(BF16)

    for i in range(4):
        loads[i].wait()
    for t in range(LEAVES_DEV):
        lanes = pl.ds(t * 128, 128)
        e_pair = split(stack(e_v[pl.ds(t, 32, stride=8), :]))
        b_pair = split(twice(basis_v[t]))
        w_pair = split(dot3(e_pair, b_pair, NN))
        for k in range(2):
            w_h[pl.ds(k * 64, 64), lanes] = w_pair[0]
            w_l[pl.ds(k * 64, 64), lanes] = w_pair[1]
    signal = [jnp.concatenate([src_v[0, t], src_v[1, t]], axis=0) for t in range(LEAVES_DEV)]
    s_pair = split(jnp.concatenate(signal, axis=1))
    dev_coef = dot3(s_pair, (w_h[...], w_l[...]), NT)
    f_high, f_low = split(f_v[...])
    f_high, f_low = dot(f_high, perm_v[...], NN), dot(f_low, perm_v[...], NN)
    rf_h[...] = twice(stack(f_high)).astype(BF16)
    rf_l[...] = twice(stack(f_low)).astype(BF16)
    d_pair = split(jnp.where(left, dev_coef, 0.0) + jnp.where(left, 0.0, dev_coef))
    up = dot3(d_pair, (rf_h[...], rf_l[...]), NT)
    table[core, z, 0:8, :] = pack(dev_coef)
    table[core, z, 8:16, :] = pack(up)
    loads[4].wait()
    for t in range(LEAVES_DEV):
        slot, j = sub * 2 + t // 4, t % 4
        b_pair = split(twice(basis_v[t]))
        t_pair = (s_pair[0][:, t * 128 : t * 128 + 128], s_pair[1][:, t * 128 : t * 128 + 128])
        gat[slot, 2 * j] = src_v[0, t]
        gat[slot, 2 * j + 1] = src_v[1, t]
        gat[slot, 8 + j] = pack(dot3(t_pair, b_pair, NT))
    for half in range(2):
        gat[sub * 2 + half, 13] = jnp.zeros((8, 128), F32)
    for t in range(LEAVES_DEV):
        for i in range(3):
            gat[sub * 2 + t // 4, 12 + i // 2, pl.ds(i % 2 * 4 + t % 4, 1), :] = pts_v[i : i + 1, t * 128 : t * 128 + 128]
    loads[5].wait()
    req_v[sub] = jnp.zeros((1, 128), jnp.int32)
    req_v[sub, :, 0:8] = dfar_v[...]

    pl.semaphore_wait(barrier, 2 * NSUB - 1)

    z_copies = []
    for i, o in enumerate(others):
        z_copies.append(
            pltpu.make_async_remote_copy(
                table.at[core, z], table.at[core, z], z_send.at[i], z_recv.at[z],
                device_id=(o * 2 + core, sub), device_id_type=MESH,
            )
        )
    for c in z_copies:
        c.start()
    req_copies = []
    for i, o in enumerate(plane):
        req_copies.append(
            pltpu.make_async_remote_copy(
                req_v.at[sub], req_v.at[sub], req_send.at[i], req_recv.at[sub],
                device_id=(leaf, o), device_id_type=MESH,
            )
        )
    for c in req_copies:
        c.start()

    def half_copy(number, slot, target):
        return pltpu.make_async_remote_copy(
            gat.at[slot], gat.at[slot], gat_send.at[number], gat_recv.at[slot],
            device_id=(leaf, target), device_id_type=MESH,
        )

    steps = (1, 3, 2)
    first = []
    for half in range(2):
        for d in steps:
            target = at_plane(0, d) if half == 0 else at_plane(d, 0)
            first.append(half_copy(len(first), sub * 2 + half, target))
    for c in first:
        c.start()
    second = []

    def pass_on(half, d):
        origin = at_plane(0, d) if half == 0 else at_plane(d, 0)
        slot = origin * 2 + half
        if d:
            pltpu.make_async_remote_copy(
                gat.at[slot], gat.at[slot], gat_send.at[0], gat_recv.at[slot], device_id=(leaf, origin), device_id_type=MESH
            ).wait_recv()
        for e in steps:
            target = at_plane(e, 0) if half == 0 else at_plane(0, e)
            c = half_copy(len(first) + len(second), slot, target)
            c.start()
            second.append(c)

    for half in range(2):
        pass_on(half, 0)

    for i in range(9, 11):
        loads[i].wait()
    for given, to_h, to_l in ((dc_v, rd_h, rd_l), (gc_v, rg_h, rg_l)):
        high, low = split(given[...])
        given[...] = dot(high, perm_v[...], NN)
        for k in range(FAR):
            to_h[:, k * 128 : k * 128 + 128] = twice(stack(given[pl.ds(k, 32, stride=8), :])).astype(BF16)
        given[...] = dot(low, perm_v[...], NN)
        for k in range(FAR):
            to_l[:, k * 128 : k * 128 + 128] = twice(stack(given[pl.ds(k, 32, stride=8), :])).astype(BF16)
    fw = dot3((rf_h[0:64, :], rf_l[0:64, :]), (w_h[...], w_l[...]), NN)
    fw_pair = split(fw)
    w_h[64:128, :] = fw_pair[0]
    w_l[64:128, :] = fw_pair[1]
    for t in range(LEAVES_DEV):
        for i in range(3):
            row = pts_v[i : i + 1, t * 128 : t * 128 + 128]
            cols_v[t, i] = jnp.broadcast_to(row, (128, 128)).T

    for d in steps:
        for half in range(2):
            pass_on(half, d)

    for i, o in enumerate(plane):
        pltpu.make_async_remote_copy(
            req_v.at[o], req_v.at[o], req_send.at[i], req_recv.at[o], device_id=(leaf, o), device_id_type=MESH
        ).wait_recv()
    to_scalar = pltpu.make_async_copy(req_v, req_s, req_loc)
    to_scalar.start()

    for i, o in enumerate(others):
        pltpu.make_async_remote_copy(
            table.at[core, o], table.at[core, o], z_send.at[i], z_recv.at[o], device_id=mate, device_id_type=MESH
        ).wait_recv()
    swap = pltpu.make_async_remote_copy(
        table.at[core], table.at[core], c_sem.at[0], c_sem.at[1], device_id=mate, device_id_type=MESH
    )
    swap.start()
    to_scalar.wait()
    for i in range(6, 9):
        loads[i].wait()
    pltpu.make_async_remote_copy(
        table.at[1 - core], table.at[1 - core], c_sem.at[0], c_sem.at[1], device_id=mate, device_id_type=MESH
    ).wait_recv()

    def answer(o, k):
        number = req_s[o, 0, k]
        row = table[(number >> 4) & 1, number >> 5, 0:8, :]
        return jnp.where(jnp.full((8, 128), number & (NSUB - 1), jnp.int32) == sub, row, 0.0)

    r_copies, p_copies = [], []
    for i, o in enumerate(plane):
        for k in range(FAR):
            r_out[o, k] = answer(o, k)
        c = pltpu.make_async_remote_copy(
            r_out.at[o], r_in.at[sub], r_send.at[i], r_recv.at[sub], device_id=(leaf, o), device_id_type=MESH
        )
        c.start()
        r_copies.append(c)
    for k in range(FAR):
        r_in[sub, k] = answer(sub, k)
    pieces = []
    for k in range(FAR):
        number = gfar_s[0, k]
        pieces.append(spread(table[number & 1, number >> 1, 8:16, :]))
    part = pack(dot3(split(jnp.concatenate(pieces, axis=1)), (rg_h[...], rg_l[...]), NT))
    p_out[...] = part
    p_in[sub] = part
    for i, o in enumerate(plane):
        c = pltpu.make_async_remote_copy(
            p_out, p_in.at[sub], p_send.at[i], p_recv.at[sub], device_id=(leaf, o), device_id_type=MESH
        )
        c.start()
        p_copies.append(c)

    for half in range(2):
        for d in range(NSUB):
            dy, dx = d // SIDE, d % SIDE
            if (dy if half == 0 else dx) == 0:
                continue
            slot = at_plane(dy, dx) * 2 + half
            pltpu.make_async_remote_copy(
                gat.at[slot], gat.at[slot], gat_send.at[0], gat_recv.at[slot], device_id=(leaf, sub), device_id_type=MESH
            ).wait_recv()
    loads[11].wait()

    def one_leaf(t, carry):
        total = jnp.zeros((16, 128), F32)
        for pair in range(NEAR // 2):
            tiles, vectors = [], []
            for k in (2 * pair, 2 * pair + 1):
                number = near_s[t, k]
                slot, j = number >> 2, number & 3
                square = DELTA_SQ
                for i in range(3):
                    along = cols_v[t, i] - gat[slot, 12 + i // 2, pl.ds(i % 2 * 4 + j, 1), :]
                    square = along * along + square
                tiles.append(lax.rsqrt(square))
                vectors.append(gat[slot, pl.ds(j * 2, 2)].reshape(16, 128))
            total = total + dot3(split(jnp.concatenate(vectors, axis=1)), split(jnp.concatenate(tiles, axis=1)), NT)
        lefts, rights = [], []
        for k in range(FAR):
            number = lfar_s[t, k]
            value = gat[number >> 2, 8 + (number & 3)]
            turned = pltpu.roll(value, 64, 1)
            lefts.append(jnp.concatenate([keep(0, value), keep(0, turned), keep(1, turned), keep(1, value)], axis=0))
            rights.append(lc_v[t, pl.ds(k, 32, stride=8), :])
        local = dot3(split(jnp.concatenate(lefts, axis=1)), split(jnp.concatenate(rights, axis=1)), NT)
        l_pair = split(local)
        field = NEAR_WEIGHT * total
        for parity in range(2):
            rows = slice(parity * 16, parity * 16 + 16)
            b_pair = split(basis_v[t, pl.ds(parity, 32, stride=2), :])
            field = field + dot3((l_pair[0][rows], l_pair[1][rows]), b_pair, NN)
        acc[t] = field
        return carry

    lax.fori_loop(0, LEAVES_DEV, one_leaf, 0)

    for i, o in enumerate(plane):
        pltpu.make_async_remote_copy(
            r_in.at[o], r_in.at[o], r_send.at[i], r_recv.at[o], device_id=(leaf, o), device_id_type=MESH
        ).wait_recv()
        pltpu.make_async_remote_copy(
            p_in.at[o], p_in.at[o], p_send.at[i], p_recv.at[o], device_id=(leaf, o), device_id_type=MESH
        ).wait_recv()
    asked = r_in[0]
    grp_local = p_in[0]
    for o in range(1, NSUB):
        asked = asked + r_in[o]
        grp_local = grp_local + p_in[o]
    dev_local = dot3(split(jnp.concatenate([spread(asked[k]) for k in range(FAR)], axis=1)), (rd_h[...], rd_l[...]), NT)
    both = split(jnp.where(left, dev_local, spread(grp_local)))
    far = dot3(both, (w_h[...], w_l[...]), NN)
    for t in range(LEAVES_DEV):
        field = acc[t] + far[:, t * 128 : t * 128 + 128]
        out[0, t] = field[0:8]
        out[1, t] = field[8:16]

    for c in z_copies + req_copies + first + second + [swap] + r_copies + p_copies:
        c.wait_send()


def body(
    sources, points, basis, leaf_transfer, dev_transfer, leaf_coupling, dev_coupling, grp_coupling, near_list, leaf_far,
    dev_far, grp_far,
):
    def rows(array):
        m = array.shape[0]
        return array.reshape(m, 8, 32, 128).transpose(0, 2, 1, 3).reshape(m, 256, 128)

    any_space = pl.BlockSpec(memory_space=pl.ANY)
    vm, sm, dma = pltpu.VMEM, pltpu.SMEM, pltpu.SemaphoreType.DMA
    result = pl.pallas_call(
        kernel,
        out_shape=jax.ShapeDtypeStruct((2, 8, 8, 128), F32),
        in_specs=[any_space] * 12,
        out_specs=pl.BlockSpec(memory_space=pltpu.VMEM),
        scratch_shapes=[
            vm((2, 8, 8, 128), F32), vm((3, 1024), F32), vm((8, 64, 128), F32), vm((256, 128), F32), vm((32, 128), F32),
            vm((8, 256, 128), F32), vm((256, 128), F32), vm((256, 128), F32), vm((1, 8), jnp.int32),
            sm((8, 8), jnp.int32), sm((8, 8), jnp.int32), sm((1, 8), jnp.int32),
            vm((128, 1024), BF16), vm((128, 1024), BF16), vm((128, 128), BF16), vm((128, 128), BF16),
            vm((128, 1024), BF16), vm((128, 1024), BF16), vm((128, 1024), BF16), vm((128, 1024), BF16),
            vm((128, 128), BF16), vm((8, 3, 128, 128), F32), vm((8, 16, 128), F32),
            vm((32, HALF_TILES, 8, 128), F32), vm((2, NZ, 16, 128), F32), vm((NSUB, 1, 128), jnp.int32), sm((NSUB, 1, 128), jnp.int32),
            vm((NSUB, FAR, 8, 128), F32), vm((NSUB, FAR, 8, 128), F32), vm((8, 128), F32), vm((NSUB, 8, 128), F32),
            dma((12,)), dma((30,)), dma((32,)), dma((15,)), dma((16,)), dma((2,)), dma((15,)), dma((16,)), dma,
            dma((15,)), dma((16,)), dma((15,)), dma((16,)),
        ],
        compiler_params=pltpu.CompilerParams(collective_id=0, has_side_effects=True, vmem_limit_bytes=48 * 1024 * 1024),
    )(
        sources.reshape(2, 8, 8, 128).transpose(0, 2, 1, 3),
        points,
        basis,
        rows(leaf_transfer[None])[0],
        dev_transfer.reshape(32, 128),
        rows(leaf_coupling),
        rows(dev_coupling)[0],
        rows(grp_coupling)[0],
        near_list, leaf_far, dev_far, grp_far,
    )
    return result.transpose(0, 2, 1, 3).reshape(16, 1024)


def solution(mesh):
    both = ("leaf", "sub")
    placed = (
        P(None, both), P(None, both), P(both, None, None), P(both, None), P(both, None), P(both, None, None),
        P(both, None, None), P("leaf", None, None), P(both, None), P(both, None), P(both, None), P("leaf", None),
    )
    return jax.shard_map(body, mesh=mesh, in_specs=placed, out_specs=P(None, both), check_vma=False)
```

time: 290 us -> 51.7 us (0.18)
  blocking collectives: 123 us -> 0 us
  waiting for transfers between devices: 98.9 us -> 0 us
  Pallas kernels: 0 us -> 42.7 us
  matrix products: 22.9 us -> 0 us
  local copies, waits for them, and re-layouts: 27.4 us -> 8.48 us
  between operations: 13.6 us -> 0.03 us
    all_gather x2 -> x0, waiting for transfers between devices: 98.2 us -> none  [the longest x1 98.2 us: body(): lax.all_gather(dev_coef[None], ('leaf', 'sub'), axis=0, tiled=True)]
    all_gather x3 -> x0, blocking collectives: 91.8 us -> none  [the longest x1 52.7 us: body(): grp_all = lax.all_gather(grp_coef[None], 'leaf', axis=0, tiled=True)]
    pallas_call x0 -> x1, Pallas kernels: none -> 42.7 us  [body(): pl.pallas_call(kernel, out_shape=jax.ShapeDtypeStruct((2, 8, 8, 128), F32...]
    psum x1 -> x0, blocking collectives: 31.4 us -> none  [body(): grp_coef = lax.psum(up_term, 'sub')]
    dot_general x19 -> x0, matrix products: 22.9 us -> none  [the longest x8 10.1 us: near_step(): jnp.einsum('tpq,vtq->vtp', kernel_tile, signal_all[:, source_leaves, :],...]
    gather x17 -> x0, local copies, waits for them, and re-layouts: 18.1 us -> none  [the longest x8 12.2 us: near_step(): kernel_tile = kernel_block(own_points, points_all[:, source_leaves, :])]
    reshape x6 -> x0, local copies, waits for them, and re-layouts: 7.16 us -> none  [the longest x1 2 us: body(): leaf_coupling.reshape(count_leaf, leaf_far.shape[1], rank_size, rank_size)]
    unnamed x22 -> x25, local copies, waits for them, and re-layouts: 2.02 us -> 8.48 us
  transfers between devices with their start and end apart: 2 -> 0, of which waited for: 1 -> 0; matrix products, arithmetic and copies ran while one was open for 16% -> 0% of each run, Pallas kernels for 0% -> 0%
where the time goes in v1:
time: 51.7 us; the launch traced here: 51.2 us
  Pallas kernels  42.7 us (83%)
  local copies, waits for them, and re-layouts  8.48 us (16%)
    pallas_call x1, Pallas kernels, body(): pl.pallas_call(kernel, out_shape=jax.ShapeDtypeStruct((2, 8, 8, 128), F32...  42.7 us
    unnamed x25, local copies, waits for them, and re-layouts  8.48 us

profile of v1, /device:TPU:1, one launch (start us, length us, event | category | flops | bytes accessed | tf_op | source)
XLA Modules:
  0.0 51.2 jit_solution(8704145607690284780)
XLA Ops:
  0.0 0.0 copy-start.9
  0.0 0.0 copy-start.8
  0.0 0.0 copy-start.10
  0.0 0.0 copy-start.11
  0.0 0.7 %copy-done.9 = s32[8,8]{1,0:T(8,128)S(1)} copy-done((s32[8,8]{1,0:T(8,128)S(1)}, s32[8,8]{1,0:T(8,128)}, u32[]{:S(2)}) %copy-start.9) | copy-done | bytes 280
  0.7 0.0 copy-done.8
  0.7 0.0 copy-done.10
  0.7 0.0 copy-done.11
  0.7 0.0 copy-start
  0.7 1.2 %copy-done = f32[8,8,4096]{2,1,0:T(8,128)S(1)} copy-done((f32[8,8,4096]{2,1,0:T(8,128)S(1)}, f32[8,8,4096]{2,1,0:T(8,128)}, u32[]{:S(2)}) %copy-start) | copy-done | bytes 1048600
  1.9 0.0 copy-start.1
  1.9 0.9 %copy-done.1 = f32[8,64,128]{2,1,0:T(8,128)S(1)} copy-done((f32[8,64,128]{2,1,0:T(8,128)S(1)}, f32[8,64,128]{2,1,0:T(8,128)}, u32[]{:S(2)}) %copy-start.1) | copy-done | bytes 262168
  2.9 0.0 copy-start.2
  2.9 0.9 %copy-done.2 = f32[8,4096]{1,0:T(8,128)S(1)} copy-done((f32[8,4096]{1,0:T(8,128)S(1)}, f32[8,4096]{1,0:T(8,128)}, u32[]{:S(2)}) %copy-start.2) | copy-done | bytes 131096
  3.8 0.0 copy-start.3
  3.8 0.9 %copy-done.3 = f32[1,8,4096]{2,1,0:T(8,128)S(1)} copy-done((f32[1,8,4096]{2,1,0:T(8,128)S(1)}, f32[1,8,4096]{2,1,0:T(8,128)}, u32[]{:S(2)}) %copy-start.3) | copy-done | bytes 131096
  4.7 0.0 copy-start.4
  4.7 0.9 %copy-done.4 = f32[1,8,4096]{2,1,0:T(8,128)S(1)} copy-done((f32[1,8,4096]{2,1,0:T(8,128)S(1)}, f32[1,8,4096]{2,1,0:T(8,128)}, u32[]{:S(2)}) %copy-start.4) | copy-done | bytes 131096
  5.6 0.0 copy-start.5
  5.6 0.8 %copy-done.5 = f32[16,1024]{1,0:T(8,128)S(1)} copy-done((f32[16,1024]{1,0:T(8,128)S(1)}, f32[16,1024]{1,0:T(8,128)}, u32[]{:S(2)}) %copy-start.5) | copy-done | bytes 65560
  6.4 0.0 copy-start.6
  6.4 0.7 %copy-done.6 = f32[3,1024]{1,0:T(4,128)S(1)} copy-done((f32[3,1024]{1,0:T(4,128)S(1)}, f32[3,1024]{1,0:T(4,128)}, u32[]{:S(2)}) %copy-start.6) | copy-done | bytes 12312
  7.2 0.0 copy-start.7
  7.2 0.7 %copy-done.7 = f32[1,4096]{1,0:T(1,128)S(1)} copy-done((f32[1,4096]{1,0:T(1,128)S(1)}, f32[1,4096]{1,0:T(1,128)}, u32[]{:S(2)}) %copy-start.7) | copy-done | bytes 16408
  7.9 42.7 %shard_map.118 = f32[2,8,8,128]{3,2,1,0:T(8,128)S(1)} custom-call(f32[2,8,8,128]{3,2,1,0:T(8,128)S(1)} %bitcast.32, f32[3,1024]{1,0:T(4,128)S(1)} %copy-done.6, f32[8,64,128]{2,1,0:T(8,128)S(1)} %copy-done.1, f32[256,128]{1,0:T(8,128)S(1)} %bitcast.29, f32[32,128]{1,0:T(8,128)S(1)} %bitcast.33, f32[8,256,128]{2,1,0:T(8,128)S(1)} %bitcast.27, ...), custom_call_target="tpu_custom_call" | custom-call | tf_op jit(solution)/shard_map/pallas_call | solution.py:336
  50.6 0.6 %copy.14 = f32[16,1024]{1,0:T(8,128)} copy(f32[16,1024]{1,0:T(8,128)S(1)} %bitcast.28) | data formatting | bytes 131072
Async XLA Ops:
  0.0 0.7 %copy-start.9 = (s32[8,8]{1,0:T(8,128)S(1)}, s32[8,8]{1,0:T(8,128)}, u32[]{:S(2)}) copy-start(s32[8,8]{1,0:T(8,128)} %lfar_hbm.1) | copy-start | bytes 772
  0.0 0.7 %copy-start.8 = (s32[8,8]{1,0:T(8,128)S(1)}, s32[8,8]{1,0:T(8,128)}, u32[]{:S(2)}) copy-start(s32[8,8]{1,0:T(8,128)} %near_hbm.1) | copy-start | bytes 772
  0.0 0.7 %copy-start.10 = (s32[1,8]{1,0:T(1,128)S(1)}, s32[1,8]{1,0:T(1,128)}, u32[]{:S(2)}) copy-start(s32[1,8]{1,0:T(1,128)} %dfar_hbm.1) | copy-start | bytes 100
  0.0 0.7 %copy-start.11 = (s32[1,8]{1,0:T(1,128)S(1)}, s32[1,8]{1,0:T(1,128)}, u32[]{:S(2)}) copy-start(s32[1,8]{1,0:T(1,128)} %gfar_hbm.1) | copy-start | bytes 100
  0.7 1.2 %copy-start = (f32[8,8,4096]{2,1,0:T(8,128)S(1)}, f32[8,8,4096]{2,1,0:T(8,128)}, u32[]{:S(2)}) copy-start(f32[8,8,4096]{2,1,0:T(8,128)} %param.17) | copy-start | bytes 3145732
  1.9 0.9 %copy-start.1 = (f32[8,64,128]{2,1,0:T(8,128)S(1)}, f32[8,64,128]{2,1,0:T(8,128)}, u32[]{:S(2)}) copy-start(f32[8,64,128]{2,1,0:T(8,128)} %basis.1) | copy-start | bytes 786436
  2.9 0.9 %copy-start.2 = (f32[8,4096]{1,0:T(8,128)S(1)}, f32[8,4096]{1,0:T(8,128)}, u32[]{:S(2)}) copy-start(f32[8,4096]{1,0:T(8,128)} %param.15) | copy-start | bytes 393220
  3.8 0.9 %copy-start.3 = (f32[1,8,4096]{2,1,0:T(8,128)S(1)}, f32[1,8,4096]{2,1,0:T(8,128)}, u32[]{:S(2)}) copy-start(f32[1,8,4096]{2,1,0:T(8,128)} %param.18) | copy-start | bytes 393220
  4.7 0.9 %copy-start.4 = (f32[1,8,4096]{2,1,0:T(8,128)S(1)}, f32[1,8,4096]{2,1,0:T(8,128)}, u32[]{:S(2)}) copy-start(f32[1,8,4096]{2,1,0:T(8,128)} %param.19) | copy-start | bytes 393220
  5.6 0.8 %copy-start.5 = (f32[16,1024]{1,0:T(8,128)S(1)}, f32[16,1024]{1,0:T(8,128)}, u32[]{:S(2)}) copy-start(f32[16,1024]{1,0:T(8,128)} %param.12) | copy-start | bytes 196612
  6.4 0.7 %copy-start.6 = (f32[3,1024]{1,0:T(4,128)S(1)}, f32[3,1024]{1,0:T(4,128)}, u32[]{:S(2)}) copy-start(f32[3,1024]{1,0:T(4,128)} %pts.1) | copy-start | bytes 36868
  7.2 0.7 %copy-start.7 = (f32[1,4096]{1,0:T(1,128)S(1)}, f32[1,4096]{1,0:T(1,128)}, u32[]{:S(2)}) copy-start(f32[1,4096]{1,0:T(1,128)} %param.16) | copy-start | bytes 49156

commit v2 on v1

--- a/solution.py
+++ b/solution.py
@@ -46,7 +46,6 @@
         return lax.rem(y + dy, SIDE) * SIDE + lax.rem(x + dx, SIDE)
 
     plane = [at_plane(d // SIDE, d % SIDE) for d in range(1, NSUB)]
-    others = [i + (i >= z).astype(jnp.int32) for i in range(NZ - 1)]
     mate = (leaf + 1 - 2 * core, sub)
 
     pairs = [
@@ -57,8 +56,12 @@
     for c in loads:
         c.start()
     barrier = pltpu.get_barrier_semaphore()
-    for o in others:
+
+    def announce(o, carry):
         pl.semaphore_signal(barrier, inc=1, device_id=(o * 2 + core, sub), device_id_type=MESH)
+        return carry
+
+    lax.fori_loop(z + 1, NZ, announce, 0)
     for o in plane:
         pl.semaphore_signal(barrier, inc=1, device_id=(leaf, o), device_id_type=MESH)
     pl.semaphore_signal(barrier, inc=1, device_id=mate, device_id_type=MESH)
@@ -108,6 +111,19 @@
     up = dot3(d_pair, (rf_h[...], rf_l[...]), NT)
     table[core, z, 0:8, :] = pack(dev_coef)
     table[core, z, 8:16, :] = pack(up)
+    pl.semaphore_wait(barrier, NSUB + z)
+
+    def z_copy(source, target):
+        return pltpu.make_async_remote_copy(
+            table.at[core, source], table.at[core, source], z_send.at[target], z_recv.at[source],
+            device_id=(target * 2 + core, sub), device_id_type=MESH,
+        )
+
+    def to_lower(o, carry):
+        z_copy(z, o).start()
+        return carry
+
+    lax.fori_loop(0, z, to_lower, 0)
     loads[4].wait()
     for t in range(LEAVES_DEV):
         slot, j = sub * 2 + t // 4, t % 4
@@ -125,18 +141,6 @@
     req_v[sub] = jnp.zeros((1, 128), jnp.int32)
     req_v[sub, :, 0:8] = dfar_v[...]
 
-    pl.semaphore_wait(barrier, 2 * NSUB - 1)
-
-    z_copies = []
-    for i, o in enumerate(others):
-        z_copies.append(
-            pltpu.make_async_remote_copy(
-                table.at[core, z], table.at[core, z], z_send.at[i], z_recv.at[z],
-                device_id=(o * 2 + core, sub), device_id_type=MESH,
-            )
-        )
-    for c in z_copies:
-        c.start()
     req_copies = []
     for i, o in enumerate(plane):
         req_copies.append(
@@ -210,10 +214,17 @@
     to_scalar = pltpu.make_async_copy(req_v, req_s, req_loc)
     to_scalar.start()
 
-    for i, o in enumerate(others):
-        pltpu.make_async_remote_copy(
-            table.at[core, o], table.at[core, o], z_send.at[i], z_recv.at[o], device_id=mate, device_id_type=MESH
-        ).wait_recv()
+    def from_higher(o, carry):
+        z_copy(o, o).wait_recv()
+        z_copy(z, o).start()
+        return carry
+
+    def from_lower(o, carry):
+        z_copy(o, o).wait_recv()
+        return carry
+
+    lax.fori_loop(z + 1, NZ, from_higher, 0)
+    lax.fori_loop(0, z, from_lower, 0)
     swap = pltpu.make_async_remote_copy(
         table.at[core], table.at[core], c_sem.at[0], c_sem.at[1], device_id=mate, device_id_type=MESH
     )
@@ -319,7 +330,13 @@
         out[0, t] = field[0:8]
         out[1, t] = field[8:16]
 
-    for c in z_copies + req_copies + first + second + [swap] + r_copies + p_copies:
+    def sent(o, carry):
+        z_copy(z, o).wait_send()
+        return carry
+
+    lax.fori_loop(0, z, sent, 0)
+    lax.fori_loop(z + 1, NZ, sent, 0)
+    for c in req_copies + first + second + [swap] + r_copies + p_copies:
         c.wait_send()
 
 
@@ -331,12 +348,12 @@
         m = array.shape[0]
         return array.reshape(m, 8, 32, 128).transpose(0, 2, 1, 3).reshape(m, 256, 128)
 
-    any_space = pl.BlockSpec(memory_space=pl.ANY)
+    in_hbm = pl.BlockSpec(memory_space=pltpu.HBM)
     vm, sm, dma = pltpu.VMEM, pltpu.SMEM, pltpu.SemaphoreType.DMA
     result = pl.pallas_call(
         kernel,
         out_shape=jax.ShapeDtypeStruct((2, 8, 8, 128), F32),
-        in_specs=[any_space] * 12,
+        in_specs=[in_hbm] * 12,
         out_specs=pl.BlockSpec(memory_space=pltpu.VMEM),
         scratch_shapes=[
             vm((2, 8, 8, 128), F32), vm((3, 1024), F32), vm((8, 64, 128), F32), vm((256, 128), F32), vm((32, 128), F32),
@@ -347,10 +364,10 @@
             vm((128, 128), BF16), vm((8, 3, 128, 128), F32), vm((8, 16, 128), F32),
             vm((32, HALF_TILES, 8, 128), F32), vm((2, NZ, 16, 128), F32), vm((NSUB, 1, 128), jnp.int32), sm((NSUB, 1, 128), jnp.int32),
             vm((NSUB, FAR, 8, 128), F32), vm((NSUB, FAR, 8, 128), F32), vm((8, 128), F32), vm((NSUB, 8, 128), F32),
-            dma((12,)), dma((30,)), dma((32,)), dma((15,)), dma((16,)), dma((2,)), dma((15,)), dma((16,)), dma,
+            dma((12,)), dma((30,)), dma((32,)), dma((16,)), dma((16,)), dma((2,)), dma((15,)), dma((16,)), dma,
             dma((15,)), dma((16,)), dma((15,)), dma((16,)),
         ],
-        compiler_params=pltpu.CompilerParams(collective_id=0, has_side_effects=True, vmem_limit_bytes=48 * 1024 * 1024),
+        compiler_params=pltpu.CompilerParams(collective_id=0, has_side_effects=True, vmem_limit_bytes=60 * 1024 * 1024),
     )(
         sources.reshape(2, 8, 8, 128).transpose(0, 2, 1, 3),
         points,

time: 51.7 us -> 41.8 us (0.81)
  the two profiles are of different devices: /device:TPU:1 before, /device:TPU:481 now
where the time goes in v2:
time: 41.8 us; the launch traced here: 41.6 us
  Pallas kernels  40.1 us (96%)
  local copies, waits for them, and re-layouts  1.47 us (4%)
    pallas_call x1, Pallas kernels, body(): pl.pallas_call(kernel, out_shape=jax.ShapeDtypeStruct((2, 8, 8, 128), F32...  40.1 us
    unnamed x1, local copies, waits for them, and re-layouts  1.47 us

profile of v2, /device:TPU:481, one launch (start us, length us, event | category | flops | bytes accessed | tf_op | source)
XLA Modules:
  0.0 41.6 jit_solution(6757930827946887496)
XLA Ops:
  0.0 40.1 %shard_map.118 = f32[2,8,8,128]{3,2,1,0:T(8,128)} custom-call(f32[2,8,8,128]{3,2,1,0:T(8,128)} %bitcast.32, f32[3,1024]{1,0:T(4,128)} %pts.1, f32[8,64,128]{2,1,0:T(8,128)} %basis.1, f32[256,128]{1,0:T(8,128)} %bitcast.29, f32[32,128]{1,0:T(8,128)} %bitcast.33, f32[8,256,128]{2,1,0:T(8,128)} %bitcast.27, f32[256,128]{1,0:T(8,128)} %bitcast.30, ...), custom_call_target="tpu_custom_call" | custom-call | tf_op jit(solution)/shard_map/pallas_call | solution.py:353
  40.1 1.5 %copy.14 = f32[16,1024]{1,0:T(8,128)} copy(f32[16,1024]{1,0:T(8,128)} %bitcast.28) | data formatting | bytes 131072

commit v3 on v2

--- a/solution.py
+++ b/solution.py
@@ -9,6 +9,7 @@
 F32, BF16 = jnp.float32, jnp.bfloat16
 DELTA_SQ = 0.01
 NZ, NSUB, SIDE = 16, 16, 4
+EARLY, FAR_Z = 4, 5
 LEAVES_DEV, NEAR, FAR = 8, 8, 8
 HALF_TILES = 14
 NEAR_WEIGHT = 1.0 / 32.0
@@ -35,7 +36,7 @@
     src_v, pts_v, basis_v, e_v, f_v, lc_v, dc_v, gc_v, dfar_v, near_s, lfar_s, gfar_s,
     w_h, w_l, rf_h, rf_l, rd_h, rd_l, rg_h, rg_l, perm_v, cols_v, acc,
     gat, table, req_v, req_s, r_out, r_in, p_out, p_in,
-    loc_sem, gat_send, gat_recv, z_send, z_recv, c_sem, req_send, req_recv, req_loc, r_send, r_recv, p_send, p_recv,
+    loc_sem, here_sem, gat_send, gat_recv, z_send, z_recv, c_sem, req_send, req_recv, req_loc, r_send, r_recv, p_send, p_recv,
 ):
     leaf = lax.axis_index("leaf")
     sub = lax.axis_index("sub")
@@ -45,8 +46,32 @@
     def at_plane(dy, dx):
         return lax.rem(y + dy, SIDE) * SIDE + lax.rem(x + dx, SIDE)
 
-    plane = [at_plane(d // SIDE, d % SIDE) for d in range(1, NSUB)]
+    ring = (0, 1, 2, 1)
+    order = sorted(range(1, NSUB), key=lambda d: -ring[d // SIDE] - ring[d % SIDE])
+    plane = [at_plane(d // SIDE, d % SIDE) for d in order]
+    up_from = jnp.where(z < EARLY, z + 1, z + FAR_Z)
+    low_end = jnp.minimum(z, EARLY)
+    peer_from = jnp.maximum(EARLY, z - FAR_Z + 1)
+    peer_next = jnp.where(z < EARLY, NZ, z + 1)
+    peer_end = jnp.minimum(NZ, z + FAR_Z)
+    late = (z >= EARLY).astype(jnp.int32)
+
+    peers = late * (z - peer_from + peer_end - 1 - z)
+
     mate = (leaf + 1 - 2 * core, sub)
+
+    barrier = pltpu.get_barrier_semaphore()
+    for o in plane:
+        pl.semaphore_signal(barrier, inc=1, device_id=(leaf, o), device_id_type=MESH)
+    pl.semaphore_signal(barrier, inc=1, device_id=mate, device_id_type=MESH)
+
+    def announce(o, carry):
+        pl.semaphore_signal(barrier, inc=1, device_id=(o * 2 + core, sub), device_id_type=MESH)
+        return carry
+
+    lax.fori_loop(peer_from, z, announce, 0)
+    lax.fori_loop(peer_next, peer_end, announce, 0)
+    lax.fori_loop(up_from, NZ, announce, 0)
 
     pairs = [
         (basis, basis_v), (e_hbm, e_v), (src, src_v), (f_hbm, f_v), (pts, pts_v), (dfar_hbm, dfar_v), (near_hbm, near_s),
@@ -55,17 +80,6 @@
     loads = [pltpu.make_async_copy(a, b, loc_sem.at[i]) for i, (a, b) in enumerate(pairs)]
     for c in loads:
         c.start()
-    barrier = pltpu.get_barrier_semaphore()
-
-    def announce(o, carry):
-        pl.semaphore_signal(barrier, inc=1, device_id=(o * 2 + core, sub), device_id_type=MESH)
-        return carry
-
-    lax.fori_loop(z + 1, NZ, announce, 0)
-    for o in plane:
-        pl.semaphore_signal(barrier, inc=1, device_id=(leaf, o), device_id_type=MESH)
-    pl.semaphore_signal(barrier, inc=1, device_id=mate, device_id_type=MESH)
-
     lane = lax.broadcasted_iota(jnp.int32, (1, 128), 1)
     left = lane < 64
 
@@ -111,19 +125,6 @@
     up = dot3(d_pair, (rf_h[...], rf_l[...]), NT)
     table[core, z, 0:8, :] = pack(dev_coef)
     table[core, z, 8:16, :] = pack(up)
-    pl.semaphore_wait(barrier, NSUB + z)
-
-    def z_copy(source, target):
-        return pltpu.make_async_remote_copy(
-            table.at[core, source], table.at[core, source], z_send.at[target], z_recv.at[source],
-            device_id=(target * 2 + core, sub), device_id_type=MESH,
-        )
-
-    def to_lower(o, carry):
-        z_copy(z, o).start()
-        return carry
-
-    lax.fori_loop(0, z, to_lower, 0)
     loads[4].wait()
     for t in range(LEAVES_DEV):
         slot, j = sub * 2 + t // 4, t % 4
@@ -141,6 +142,51 @@
     req_v[sub] = jnp.zeros((1, 128), jnp.int32)
     req_v[sub, :, 0:8] = dfar_v[...]
 
+    pl.semaphore_wait(barrier, NSUB + low_end + late * jnp.maximum(0, z - FAR_Z - EARLY + 1) + peers)
+
+    def z_copy(source, target):
+        return pltpu.make_async_remote_copy(
+            table.at[core, source], table.at[core, source], z_send.at[target], z_recv.at[source],
+            device_id=(target * 2 + core, sub), device_id_type=MESH,
+        )
+
+    def send_z(o, carry):
+        z_copy(z, o).start()
+        return carry
+
+    def send_down(o, carry):
+        pl.semaphore_signal(here_sem.at[z], inc=1, device_id=(o * 2 + core, sub), device_id_type=MESH)
+        return send_z(o, carry)
+
+    lax.fori_loop(0, low_end, send_down, 0)
+    lax.fori_loop(EARLY, z - FAR_Z + 1, send_down, 0)
+    lax.fori_loop(peer_from, z, send_z, 0)
+    lax.fori_loop(peer_next, peer_end, send_z, 0)
+
+    def half_copy(number, slot, target):
+        return pltpu.make_async_remote_copy(
+            gat.at[slot], gat.at[slot], gat_send.at[number], gat_recv.at[slot],
+            device_id=(leaf, target), device_id_type=MESH,
+        )
+
+    sends = []
+
+    def pass_on(half, d, steps):
+        if d is None:
+            slot, targets = sub * 2 + half, [at_plane(0, e) if half == 0 else at_plane(e, 0) for e in steps]
+        else:
+            origin = at_plane(0, d) if half == 0 else at_plane(d, 0)
+            slot, targets = origin * 2 + half, [at_plane(e, 0) if half == 0 else at_plane(0, e) for e in steps]
+            if d:
+                half_copy(0, slot, origin).wait_recv()
+        for target in targets:
+            c = half_copy(len(sends), slot, target)
+            c.start()
+            sends.append(c)
+
+    for d in (None, 0):
+        for half in range(2):
+            pass_on(half, d, (1, 3, 2))
     req_copies = []
     for i, o in enumerate(plane):
         req_copies.append(
@@ -152,38 +198,6 @@
     for c in req_copies:
         c.start()
 
-    def half_copy(number, slot, target):
-        return pltpu.make_async_remote_copy(
-            gat.at[slot], gat.at[slot], gat_send.at[number], gat_recv.at[slot],
-            device_id=(leaf, target), device_id_type=MESH,
-        )
-
-    steps = (1, 3, 2)
-    first = []
-    for half in range(2):
-        for d in steps:
-            target = at_plane(0, d) if half == 0 else at_plane(d, 0)
-            first.append(half_copy(len(first), sub * 2 + half, target))
-    for c in first:
-        c.start()
-    second = []
-
-    def pass_on(half, d):
-        origin = at_plane(0, d) if half == 0 else at_plane(d, 0)
-        slot = origin * 2 + half
-        if d:
-            pltpu.make_async_remote_copy(
-                gat.at[slot], gat.at[slot], gat_send.at[0], gat_recv.at[slot], device_id=(leaf, origin), device_id_type=MESH
-            ).wait_recv()
-        for e in steps:
-            target = at_plane(e, 0) if half == 0 else at_plane(0, e)
-            c = half_copy(len(first) + len(second), slot, target)
-            c.start()
-            second.append(c)
-
-    for half in range(2):
-        pass_on(half, 0)
-
     for i in range(9, 11):
         loads[i].wait()
     for given, to_h, to_l in ((dc_v, rd_h, rd_l), (gc_v, rg_h, rg_l)):
@@ -194,6 +208,9 @@
         given[...] = dot(low, perm_v[...], NN)
         for k in range(FAR):
             to_l[:, k * 128 : k * 128 + 128] = twice(stack(given[pl.ds(k, 32, stride=8), :])).astype(BF16)
+    for d in (1, 3):
+        for half in range(2):
+            pass_on(half, d, (1, 3, 2))
     fw = dot3((rf_h[0:64, :], rf_l[0:64, :]), (w_h[...], w_l[...]), NN)
     fw_pair = split(fw)
     w_h[64:128, :] = fw_pair[0]
@@ -203,9 +220,8 @@
             row = pts_v[i : i + 1, t * 128 : t * 128 + 128]
             cols_v[t, i] = jnp.broadcast_to(row, (128, 128)).T
 
-    for d in steps:
-        for half in range(2):
-            pass_on(half, d)
+    for half in range(2):
+        pass_on(half, 2, (1, 3, 2))
 
     for i, o in enumerate(plane):
         pltpu.make_async_remote_copy(
@@ -214,17 +230,20 @@
     to_scalar = pltpu.make_async_copy(req_v, req_s, req_loc)
     to_scalar.start()
 
-    def from_higher(o, carry):
-        z_copy(o, o).wait_recv()
-        z_copy(z, o).start()
-        return carry
-
-    def from_lower(o, carry):
+    def send_up(o, carry):
+        pl.semaphore_wait(here_sem.at[o], 1)
+        return send_z(o, carry)
+
+    def received(o, carry):
         z_copy(o, o).wait_recv()
         return carry
 
-    lax.fori_loop(z + 1, NZ, from_higher, 0)
-    lax.fori_loop(0, z, from_lower, 0)
+    lax.fori_loop(up_from, NZ, send_up, 0)
+    lax.fori_loop(up_from, NZ, received, 0)
+    lax.fori_loop(peer_from, z, received, 0)
+    lax.fori_loop(peer_next, peer_end, received, 0)
+    lax.fori_loop(0, low_end, received, 0)
+    lax.fori_loop(EARLY, z - FAR_Z + 1, received, 0)
     swap = pltpu.make_async_remote_copy(
         table.at[core], table.at[core], c_sem.at[0], c_sem.at[1], device_id=mate, device_id_type=MESH
     )
@@ -336,7 +355,7 @@
 
     lax.fori_loop(0, z, sent, 0)
     lax.fori_loop(z + 1, NZ, sent, 0)
-    for c in req_copies + first + second + [swap] + r_copies + p_copies:
+    for c in req_copies + sends + [swap] + r_copies + p_copies:
         c.wait_send()
 
 
@@ -352,7 +371,7 @@
     vm, sm, dma = pltpu.VMEM, pltpu.SMEM, pltpu.SemaphoreType.DMA
     result = pl.pallas_call(
         kernel,
-        out_shape=jax.ShapeDtypeStruct((2, 8, 8, 128), F32),
+        out_shape=pltpu.VMEM((2, 8, 8, 128), F32),
         in_specs=[in_hbm] * 12,
         out_specs=pl.BlockSpec(memory_space=pltpu.VMEM),
         scratch_shapes=[
@@ -364,7 +383,7 @@
             vm((128, 128), BF16), vm((8, 3, 128, 128), F32), vm((8, 16, 128), F32),
             vm((32, HALF_TILES, 8, 128), F32), vm((2, NZ, 16, 128), F32), vm((NSUB, 1, 128), jnp.int32), sm((NSUB, 1, 128), jnp.int32),
             vm((NSUB, FAR, 8, 128), F32), vm((NSUB, FAR, 8, 128), F32), vm((8, 128), F32), vm((NSUB, 8, 128), F32),
-            dma((12,)), dma((30,)), dma((32,)), dma((16,)), dma((16,)), dma((2,)), dma((15,)), dma((16,)), dma,
+            dma((12,)), pltpu.SemaphoreType.REGULAR((NZ,)), dma((30,)), dma((32,)), dma((16,)), dma((16,)), dma((2,)), dma((15,)), dma((16,)), dma,
             dma((15,)), dma((16,)), dma((15,)), dma((16,)),
         ],
         compiler_params=pltpu.CompilerParams(collective_id=0, has_side_effects=True, vmem_limit_bytes=60 * 1024 * 1024),

time: 41.8 us -> 38.3 us (0.916)
  Pallas kernels: 40.1 us -> 37.5 us
  local copies, waits for them, and re-layouts: 1.47 us -> 0.63 us
    pallas_call x1, Pallas kernels: 40.1 us -> 37.5 us  [body(): pl.pallas_call(kernel, out_shape=pltpu.VMEM((2, 8, 8, 128), F32), in_spec...]
    unnamed x1, local copies, waits for them, and re-layouts: 1.47 us -> 0.63 us
where the time goes in v3:
time: 38.3 us; the launch traced here: 38.1 us
  Pallas kernels  37.5 us (98%)
  local copies, waits for them, and re-layouts  0.63 us (2%)
    pallas_call x1, Pallas kernels, body(): pl.pallas_call(kernel, out_shape=pltpu.VMEM((2, 8, 8, 128), F32), in_spec...  37.5 us

profile of v3, /device:TPU:481, one launch (start us, length us, event | category | flops | bytes accessed | tf_op | source)
XLA Modules:
  0.0 38.1 jit_solution(9546780659371093851)
XLA Ops:
  0.0 37.5 %shard_map.118 = f32[2,8,8,128]{3,2,1,0:T(8,128)S(1)} custom-call(f32[2,8,8,128]{3,2,1,0:T(8,128)} %bitcast.32, f32[3,1024]{1,0:T(4,128)} %pts.1, f32[8,64,128]{2,1,0:T(8,128)} %basis.1, f32[256,128]{1,0:T(8,128)} %bitcast.29, f32[32,128]{1,0:T(8,128)} %bitcast.33, f32[8,256,128]{2,1,0:T(8,128)} %bitcast.28, f32[256,128]{1,0:T(8,128)} %bitcast.30, ...), custom_call_target="tpu_custom_call" | custom-call | tf_op jit(solution)/shard_map/pallas_call | solution.py:372
  37.5 0.6 %copy.14 = f32[16,1024]{1,0:T(8,128)} copy(f32[16,1024]{1,0:T(8,128)S(1)} %bitcast.27) | data formatting | bytes 131072

commit v4 on v3

--- a/solution.py
+++ b/solution.py
@@ -9,7 +9,7 @@
 F32, BF16 = jnp.float32, jnp.bfloat16
 DELTA_SQ = 0.01
 NZ, NSUB, SIDE = 16, 16, 4
-EARLY, FAR_Z = 4, 5
+EARLY, FAR_Z, NEAR_Z = 4, 9, 5
 LEAVES_DEV, NEAR, FAR = 8, 8, 8
 HALF_TILES = 14
 NEAR_WEIGHT = 1.0 / 32.0
@@ -27,7 +27,9 @@
 
 
 def dot3(a, b, dims):
-    return dot(a[0], b[0], dims) + (dot(a[1], b[0], dims) + dot(a[0], b[1], dims))
+    m = a[0].shape[0]
+    both = dot(jnp.concatenate(a, axis=0), b[0], dims)
+    return both[:m] + (both[m:] + dot(a[0], b[1], dims))
 
 
 def kernel(
@@ -36,7 +38,7 @@
     src_v, pts_v, basis_v, e_v, f_v, lc_v, dc_v, gc_v, dfar_v, near_s, lfar_s, gfar_s,
     w_h, w_l, rf_h, rf_l, rd_h, rd_l, rg_h, rg_l, perm_v, cols_v, acc,
     gat, table, req_v, req_s, r_out, r_in, p_out, p_in,
-    loc_sem, here_sem, gat_send, gat_recv, z_send, z_recv, c_sem, req_send, req_recv, req_loc, r_send, r_recv, p_send, p_recv,
+    loc_sem, here_sem, step_sem, gat_send, gat_recv, z_send, z_recv, c_sem, req_send, req_recv, req_loc, r_send, r_recv, p_send, p_recv,
 ):
     leaf = lax.axis_index("leaf")
     sub = lax.axis_index("sub")
@@ -49,14 +51,16 @@
     ring = (0, 1, 2, 1)
     order = sorted(range(1, NSUB), key=lambda d: -ring[d // SIDE] - ring[d % SIDE])
     plane = [at_plane(d // SIDE, d % SIDE) for d in order]
+    late = (z >= EARLY).astype(jnp.int32)
     up_from = jnp.where(z < EARLY, z + 1, z + FAR_Z)
     low_end = jnp.minimum(z, EARLY)
-    peer_from = jnp.maximum(EARLY, z - FAR_Z + 1)
-    peer_next = jnp.where(z < EARLY, NZ, z + 1)
-    peer_end = jnp.minimum(NZ, z + FAR_Z)
-    late = (z >= EARLY).astype(jnp.int32)
-
-    peers = late * (z - peer_from + peer_end - 1 - z)
+    near_from = jnp.maximum(EARLY, z - NEAR_Z + 1)
+    near_next = jnp.where(z < EARLY, NZ, z + 1)
+    near_end = jnp.minimum(NZ, z + NEAR_Z)
+    mid_from = jnp.maximum(EARLY, z - FAR_Z + 1)
+    mid_next = jnp.where(z < EARLY, NZ, z + NEAR_Z)
+    mid_end = jnp.minimum(NZ, z + FAR_Z)
+    peers = late * (near_end - 1 - near_from)
 
     mate = (leaf + 1 - 2 * core, sub)
 
@@ -69,8 +73,8 @@
         pl.semaphore_signal(barrier, inc=1, device_id=(o * 2 + core, sub), device_id_type=MESH)
         return carry
 
-    lax.fori_loop(peer_from, z, announce, 0)
-    lax.fori_loop(peer_next, peer_end, announce, 0)
+    lax.fori_loop(near_from, z, announce, 0)
+    lax.fori_loop(near_next, near_end, announce, 0)
     lax.fori_loop(up_from, NZ, announce, 0)
 
     pairs = [
@@ -160,8 +164,16 @@
 
     lax.fori_loop(0, low_end, send_down, 0)
     lax.fori_loop(EARLY, z - FAR_Z + 1, send_down, 0)
-    lax.fori_loop(peer_from, z, send_z, 0)
-    lax.fori_loop(peer_next, peer_end, send_z, 0)
+
+    def tell(o, carry):
+        pl.semaphore_signal(step_sem, inc=1, device_id=(o * 2 + core, sub), device_id_type=MESH)
+        return carry
+
+    step = NEAR_Z - 1
+    lax.fori_loop(jnp.where(z - step < EARLY, NZ, z - step), z - step + 1, tell, 0)
+    lax.fori_loop(jnp.where(z < EARLY, NZ, z + step), jnp.minimum(NZ, z + step + 1), tell, 0)
+    lax.fori_loop(near_from, z, send_z, 0)
+    lax.fori_loop(near_next, near_end, send_z, 0)
 
     def half_copy(number, slot, target):
         return pltpu.make_async_remote_copy(
@@ -211,6 +223,14 @@
     for d in (1, 3):
         for half in range(2):
             pass_on(half, d, (1, 3, 2))
+    told = (z - step >= EARLY).astype(jnp.int32) + late * (z + step < NZ).astype(jnp.int32)
+
+    @pl.when(told > 0)
+    def _():
+        pl.semaphore_wait(step_sem, told)
+
+    lax.fori_loop(mid_from, z - NEAR_Z + 1, send_z, 0)
+    lax.fori_loop(mid_next, mid_end, send_z, 0)
     fw = dot3((rf_h[0:64, :], rf_l[0:64, :]), (w_h[...], w_l[...]), NN)
     fw_pair = split(fw)
     w_h[64:128, :] = fw_pair[0]
@@ -240,8 +260,10 @@
 
     lax.fori_loop(up_from, NZ, send_up, 0)
     lax.fori_loop(up_from, NZ, received, 0)
-    lax.fori_loop(peer_from, z, received, 0)
-    lax.fori_loop(peer_next, peer_end, received, 0)
+    lax.fori_loop(near_from, z, received, 0)
+    lax.fori_loop(near_next, near_end, received, 0)
+    lax.fori_loop(mid_from, z - NEAR_Z + 1, received, 0)
+    lax.fori_loop(mid_next, mid_end, received, 0)
     lax.fori_loop(0, low_end, received, 0)
     lax.fori_loop(EARLY, z - FAR_Z + 1, received, 0)
     swap = pltpu.make_async_remote_copy(
@@ -383,7 +405,7 @@
             vm((128, 128), BF16), vm((8, 3, 128, 128), F32), vm((8, 16, 128), F32),
             vm((32, HALF_TILES, 8, 128), F32), vm((2, NZ, 16, 128), F32), vm((NSUB, 1, 128), jnp.int32), sm((NSUB, 1, 128), jnp.int32),
             vm((NSUB, FAR, 8, 128), F32), vm((NSUB, FAR, 8, 128), F32), vm((8, 128), F32), vm((NSUB, 8, 128), F32),
-            dma((12,)), pltpu.SemaphoreType.REGULAR((NZ,)), dma((30,)), dma((32,)), dma((16,)), dma((16,)), dma((2,)), dma((15,)), dma((16,)), dma,
+            dma((12,)), pltpu.SemaphoreType.REGULAR((NZ,)), pltpu.SemaphoreType.REGULAR, dma((30,)), dma((32,)), dma((16,)), dma((16,)), dma((2,)), dma((15,)), dma((16,)), dma,
             dma((15,)), dma((16,)), dma((15,)), dma((16,)),
         ],
         compiler_params=pltpu.CompilerParams(collective_id=0, has_side_effects=True, vmem_limit_bytes=60 * 1024 * 1024),

time: 38.3 us -> 36.9 us (0.963)
  Pallas kernels: 37.5 us -> 35.7 us
    pallas_call x1, Pallas kernels: 37.5 us -> 35.7 us  [body(): pl.pallas_call(kernel, out_shape=pltpu.VMEM((2, 8, 8, 128), F32), in_spec...]
where the time goes in v4:
time: 36.9 us; the launch traced here: 36.4 us
  Pallas kernels  35.7 us (97%)
  local copies, waits for them, and re-layouts  0.63 us (2%)
    pallas_call x1, Pallas kernels, body(): pl.pallas_call(kernel, out_shape=pltpu.VMEM((2, 8, 8, 128), F32), in_spec...  35.7 us

profile of v4, /device:TPU:481, one launch (start us, length us, event | category | flops | bytes accessed | tf_op | source)
XLA Modules:
  0.0 36.4 jit_solution(11798247571974609221)
XLA Ops:
  0.0 35.7 %shard_map.118 = f32[2,8,8,128]{3,2,1,0:T(8,128)S(1)} custom-call(f32[2,8,8,128]{3,2,1,0:T(8,128)} %bitcast.32, f32[3,1024]{1,0:T(4,128)} %pts.1, f32[8,64,128]{2,1,0:T(8,128)} %basis.1, f32[256,128]{1,0:T(8,128)} %bitcast.29, f32[32,128]{1,0:T(8,128)} %bitcast.33, f32[8,256,128]{2,1,0:T(8,128)} %bitcast.28, f32[256,128]{1,0:T(8,128)} %bitcast.30, ...), custom_call_target="tpu_custom_call" | custom-call | tf_op jit(solution)/shard_map/pallas_call | solution.py:394
  35.7 0.6 %copy.14 = f32[16,1024]{1,0:T(8,128)} copy(f32[16,1024]{1,0:T(8,128)S(1)} %bitcast.27) | data formatting | bytes 131072

commit v5 on v4

--- a/solution.py
+++ b/solution.py
@@ -277,22 +277,7 @@
         table.at[1 - core], table.at[1 - core], c_sem.at[0], c_sem.at[1], device_id=mate, device_id_type=MESH
     ).wait_recv()
 
-    def answer(o, k):
-        number = req_s[o, 0, k]
-        row = table[(number >> 4) & 1, number >> 5, 0:8, :]
-        return jnp.where(jnp.full((8, 128), number & (NSUB - 1), jnp.int32) == sub, row, 0.0)
-
     r_copies, p_copies = [], []
-    for i, o in enumerate(plane):
-        for k in range(FAR):
-            r_out[o, k] = answer(o, k)
-        c = pltpu.make_async_remote_copy(
-            r_out.at[o], r_in.at[sub], r_send.at[i], r_recv.at[sub], device_id=(leaf, o), device_id_type=MESH
-        )
-        c.start()
-        r_copies.append(c)
-    for k in range(FAR):
-        r_in[sub, k] = answer(sub, k)
     pieces = []
     for k in range(FAR):
         number = gfar_s[0, k]
@@ -307,6 +292,21 @@
         c.start()
         p_copies.append(c)
 
+    def answer(o, k):
+        number = req_s[o, 0, k]
+        row = table[(number >> 4) & 1, number >> 5, 0:8, :]
+        return jnp.where(jnp.full((8, 128), number & (NSUB - 1), jnp.int32) == sub, row, 0.0)
+
+    for i, o in enumerate(plane):
+        for k in range(FAR):
+            r_out[o, k] = answer(o, k)
+        c = pltpu.make_async_remote_copy(
+            r_out.at[o], r_in.at[sub], r_send.at[i], r_recv.at[sub], device_id=(leaf, o), device_id_type=MESH
+        )
+        c.start()
+        r_copies.append(c)
+    for k in range(FAR):
+        r_in[sub, k] = answer(sub, k)
     for half in range(2):
         for d in range(NSUB):
             dy, dx = d // SIDE, d % SIDE

time: 36.9 us -> 36.6 us (level)
  no operation moved by 1% of the time
where the time goes in v5:
time: 36.6 us; the launch traced here: 36.4 us
  Pallas kernels  35.8 us (98%)
  local copies, waits for them, and re-layouts  0.63 us (2%)
    pallas_call x1, Pallas kernels, body(): pl.pallas_call(kernel, out_shape=pltpu.VMEM((2, 8, 8, 128), F32), in_spec...  35.8 us

profile of v5, /device:TPU:481, one launch (start us, length us, event | category | flops | bytes accessed | tf_op | source)
XLA Modules:
  0.0 36.4 jit_solution(3636030414058582111)
XLA Ops:
  0.0 35.8 %shard_map.118 = f32[2,8,8,128]{3,2,1,0:T(8,128)S(1)} custom-call(f32[2,8,8,128]{3,2,1,0:T(8,128)} %bitcast.32, f32[3,1024]{1,0:T(4,128)} %pts.1, f32[8,64,128]{2,1,0:T(8,128)} %basis.1, f32[256,128]{1,0:T(8,128)} %bitcast.29, f32[32,128]{1,0:T(8,128)} %bitcast.33, f32[8,256,128]{2,1,0:T(8,128)} %bitcast.28, f32[256,128]{1,0:T(8,128)} %bitcast.30, ...), custom_call_target="tpu_custom_call" | custom-call | tf_op jit(solution)/shard_map/pallas_call | solution.py:394
  35.8 0.6 %copy.14 = f32[16,1024]{1,0:T(8,128)} copy(f32[16,1024]{1,0:T(8,128)S(1)} %bitcast.27) | data formatting | bytes 131072

commit v6 on v5

--- a/solution.py
+++ b/solution.py
@@ -9,7 +9,7 @@
 F32, BF16 = jnp.float32, jnp.bfloat16
 DELTA_SQ = 0.01
 NZ, NSUB, SIDE = 16, 16, 4
-EARLY, FAR_Z, NEAR_Z = 4, 9, 5
+EARLY, FAR_Z, NEAR_Z = 6, 9, 5
 LEAVES_DEV, NEAR, FAR = 8, 8, 8
 HALF_TILES = 14
 NEAR_WEIGHT = 1.0 / 32.0

time: 36.6 us -> 36.6 us (level)
  no operation moved by 1% of the time
where the time goes in v6:
time: 36.6 us; the launch traced here: 36.4 us
  Pallas kernels  35.8 us (98%)
  local copies, waits for them, and re-layouts  0.63 us (2%)
    pallas_call x1, Pallas kernels, body(): pl.pallas_call(kernel, out_shape=pltpu.VMEM((2, 8, 8, 128), F32), in_spec...  35.8 us

profile of v6, /device:TPU:481, one launch (start us, length us, event | category | flops | bytes accessed | tf_op | source)
XLA Modules:
  0.0 36.4 jit_solution(5134130958699340156)
XLA Ops:
  0.0 35.8 %shard_map.118 = f32[2,8,8,128]{3,2,1,0:T(8,128)S(1)} custom-call(f32[2,8,8,128]{3,2,1,0:T(8,128)} %bitcast.32, f32[3,1024]{1,0:T(4,128)} %pts.1, f32[8,64,128]{2,1,0:T(8,128)} %basis.1, f32[256,128]{1,0:T(8,128)} %bitcast.29, f32[32,128]{1,0:T(8,128)} %bitcast.33, f32[8,256,128]{2,1,0:T(8,128)} %bitcast.28, f32[256,128]{1,0:T(8,128)} %bitcast.30, ...), custom_call_target="tpu_custom_call" | custom-call | tf_op jit(solution)/shard_map/pallas_call | solution.py:394
  35.8 0.6 %copy.14 = f32[16,1024]{1,0:T(8,128)} copy(f32[16,1024]{1,0:T(8,128)S(1)} %bitcast.27) | data formatting | bytes 131072
